TPU v7x, 128 devices: a whole 4x4x4 slice. The times are simulated.
128 devices in a mesh: group: 8 (over z, core), member: 16 (over x, y).
Axes of the slice: x: 4, y: 4, z: 4, core: 2. Of those that a mesh axis runs over, the one named last changes fastest.
Arguments:
- query_feat: bfloat16 [16384, 4096], P(('group', 'member'))
- code_feat: bfloat16 [16384, 4096], P(('group', 'member'))
- projection: bfloat16 [4096, 1024], replicated
- hard_ids: int32 [128, 16], P(('group', 'member')), may hold values from 0 to 255, as said below
- loss_weight: float32 [16384], P(('group', 'member')), may hold values from 1 to 4
Outputs:
- query_grad: bfloat16 [16384, 4096], P(('group', 'member'))
- code_grad: bfloat16 [16384, 4096], P(('group', 'member'))
- projection_grad: float32 [4096, 1024], P(('group', 'member'))
Inputs may be any that keep to these rules, and one draw needn't show every extreme that they name: `hard_ids`: entry (owner device g * 16 + m) * 2 + slot names code rows of that device. A row names 16 different blocks, none of its own group; at most 4 of them lie in one group, and exactly 4 in some group of every row.
All inputs are finite; a program needn't handle non-finite values.
Results may differ from a plain program's by a relative error of at most 0.02.
Values may be sent and summed in bfloat16 or wider, within the bound.
A program may use at most 128 MiB of HBM per device.

v0:
```python
import jax
import jax.numpy as jnp
from jax import lax
from jax.sharding import PartitionSpec as P

CB = 64
inverse_temp = 120.0
epsilon = 1e-06


def embed(features, projection):
    values = jnp.dot(features, projection, preferred_element_type=jnp.float32)
    inverse = lax.rsqrt(jnp.sum(values * values, axis=1) + epsilon)
    unit_vec = values * inverse[:, None]
    return (unit_vec, inverse, unit_vec.astype(jnp.bfloat16))


def norm_back(upstream, unit_vec, inverse):
    inner_prod = jnp.sum(unit_vec * upstream, axis=1, keepdims=True)
    return (inverse[:, None] * (upstream - unit_vec * inner_prod)).astype(jnp.bfloat16)


def body(query_feat, code_feat, projection, hard_ids, loss_weight):
    groups = lax.axis_size("group")
    members = lax.axis_size("member")
    member_index = lax.axis_index("member")
    queries_dev = query_feat.shape[0]
    emb_width = projection.shape[1]
    count_hard = hard_ids.shape[1]
    slot_count = queries_dev // CB
    per_group = members * slot_count
    capacity = 2 * count_hard // groups
    q_unit, q_inv, q_emb = embed(query_feat, projection)
    c_unit, c_inv, c_emb = embed(code_feat, projection)
    group_codes = lax.all_gather(c_emb, "member", axis=0, tiled=True)
    code_blocks = group_codes.reshape(per_group, CB, emb_width)
    wanted = hard_ids[0]
    owner_group = wanted // per_group
    local_block = wanted % per_group
    request_order = jnp.arange(count_hard, dtype=jnp.int32)
    same_group = (owner_group[:, None] == owner_group[None, :]) & (
        request_order[None, :] < request_order[:, None]
    )
    slot_place = jnp.sum(same_group.astype(jnp.int32), axis=1)
    pick_group = (owner_group[:, None] == jnp.arange(groups, dtype=jnp.int32)[None, :]).astype(
        jnp.int32
    )
    pick_place = (slot_place[:, None] == jnp.arange(capacity, dtype=jnp.int32)[None, :]).astype(
        jnp.int32
    )
    request_table = (
        jnp.sum(
            pick_group[:, :, None] * (pick_place * (local_block + 1)[:, None])[:, None, :], axis=0
        )
        - 1
    )
    asked_blocks = lax.all_to_all(request_table, "group", split_axis=0, concat_axis=0, tiled=True)
    asked_valid = asked_blocks >= 0
    picked = (
        code_blocks[jnp.clip(asked_blocks, 0, per_group - 1)]
        * asked_valid.astype(jnp.bfloat16)[:, :, None, None]
    )
    group_scores = inverse_temp * jnp.einsum(
        "qe,ke->qk", q_emb, group_codes, preferred_element_type=jnp.float32
    )
    offsets = jnp.arange(queries_dev, dtype=jnp.int32)
    columns = jnp.arange(members * queries_dev, dtype=jnp.int32)
    positive = (columns[None, :] == (member_index * queries_dev + offsets)[:, None]).astype(
        jnp.float32
    )
    factor = loss_weight * inverse_temp
    fetched = lax.all_to_all(picked, "group", split_axis=0, concat_axis=0, tiled=True).reshape(
        groups * capacity * CB, emb_width
    )
    table_valid = jnp.broadcast_to(
        (request_table >= 0)[:, :, None], (groups, capacity, CB)
    ).reshape(-1)
    hard_scores = jnp.where(
        table_valid[None, :],
        inverse_temp * jnp.einsum("qe,ke->qk", q_emb, fetched, preferred_element_type=jnp.float32),
        -jnp.inf,
    )
    row_max = jnp.maximum(jnp.max(group_scores, axis=1), jnp.max(hard_scores, axis=1))
    row_sum = jnp.sum(jnp.exp(group_scores - row_max[:, None]), axis=1) + jnp.sum(
        jnp.exp(hard_scores - row_max[:, None]), axis=1
    )
    log_total = row_max + jnp.log(row_sum)
    grad_hard = (factor[:, None] * jnp.exp(hard_scores - log_total[:, None])).astype(jnp.bfloat16)
    hard_delta = jnp.einsum("qk,ke->qe", grad_hard, fetched, preferred_element_type=jnp.float32)
    outgoing = jnp.einsum("qk,qe->ke", grad_hard, q_emb, preferred_element_type=jnp.float32).astype(
        jnp.bfloat16
    )
    returned = lax.all_to_all(
        outgoing.reshape(groups, capacity, CB, emb_width),
        "group",
        split_axis=0,
        concat_axis=0,
        tiled=True,
    )
    grad_group = (factor[:, None] * (jnp.exp(group_scores - log_total[:, None]) - positive)).astype(
        jnp.bfloat16
    )
    query_delta = (
        jnp.einsum("qk,ke->qe", grad_group, group_codes, preferred_element_type=jnp.float32)
        + hard_delta
    )
    hit_table = (
        asked_blocks.reshape(-1)[:, None] == jnp.arange(per_group, dtype=jnp.int32)[None, :]
    ).astype(jnp.bfloat16)
    hard_sum = jnp.einsum(
        "rj,rx->jx",
        hit_table,
        returned.reshape(groups * capacity, CB * emb_width),
        preferred_element_type=jnp.float32,
    )
    code_terms = jnp.einsum(
        "qk,qe->ke", grad_group, q_emb, preferred_element_type=jnp.float32
    ) + hard_sum.reshape(members * queries_dev, emb_width)
    code_delta = lax.psum_scatter(
        code_terms.astype(jnp.bfloat16), "member", scatter_dimension=0, tiled=True
    ).astype(jnp.float32)
    dz_query = norm_back(query_delta, q_unit, q_inv)
    dz_code = norm_back(code_delta, c_unit, c_inv)
    query_grad = jnp.einsum(
        "qe,de->qd", dz_query, projection, preferred_element_type=jnp.float32
    ).astype(jnp.bfloat16)
    code_grad = jnp.einsum(
        "qe,de->qd", dz_code, projection, preferred_element_type=jnp.float32
    ).astype(jnp.bfloat16)
    projection_grad = lax.psum_scatter(
        jnp.einsum("qd,qe->de", query_feat, dz_query, preferred_element_type=jnp.float32)
        + jnp.einsum("qd,qe->de", code_feat, dz_code, preferred_element_type=jnp.float32),
        ("group", "member"),
        scatter_dimension=0,
        tiled=True,
    )
    return (query_grad, code_grad, projection_grad)


def solution(mesh):
    return jax.shard_map(
        body,
        mesh=mesh,
        in_specs=(
            P(("group", "member"), None),
            P(("group", "member"), None),
            P(),
            P(("group", "member"), None),
            P(("group", "member")),
        ),
        out_specs=(
            P(("group", "member"), None),
            P(("group", "member"), None),
            P(("group", "member"), None),
        ),
        check_vma=False,
    )
```

profile of v0, /device:TPU:0, one launch (start us, length us, event | category | flops | bytes accessed | tf_op | source)
XLA Modules:
  0.0 1007.8 jit_solution(13707422682799377687)
XLA Ops:
  7.2 5.1 multiply_reduce_fusion.1
  14.5 10.5 %all_to_all.16 = s32[8,1,4]{2,1,0:T(1,128)S(1)} all-to-all(s32[8,1,4]{2,1,0:T(1,128)S(1)} %copy.33), channel_id=1, replica_groups=mesh['group'=8,'member'=16] {'group'}, dimensions={0} | all-to-all | bytes 256 | tf_op jit(solution)/shard_map/all_to_all | solution.py:57
  25.3 42.7 %all-gather.2.cloned.1.call-done = bf16[2048,1024]{1,0:T(8,128)(2,1)} async-done(((bf16[128,1024]{1,0:T(8,128)(2,1)}), bf16[2048,1024]{1,0:T(8,128)(2,1)}) %all-gather.2.cloned.1.call-update) | async-done | bytes 4194320 | tf_op jit(solution)/shard_map/all_gather | solution.py:35
  68.0 5.0 gather_fusion
  73.0 4.5 broadcast_multiply_fusion
  77.4 4.6 all-to-all-start.1
  82.3 4.9 multiply_reduce_fusion.2
  89.6 42.0 %all-to-all-done.1 = bf16[8,4,64,1024]{3,2,1,0:T(8,128)(2,1)} async-done(((bf16[8,4,64,1024]{3,2,1,0:T(8,128)(2,1)}), bf16[8,4,64,1024]{3,2,1,0:T(8,128)(2,1)}, u32[]{:S(2)}, u32[]{:S(2)}) %all-to-all-start.1) | async-done | bytes 4194336 | tf_op jit(solution)/shard_map/all_to_all | solution.py:72
  131.6 3.8 fusion.14
  135.9 3.4 convolution_convert_fusion.2
  139.2 4.5 all-to-all-start.2
  145.3 48.2 %all-to-all-done.2 = bf16[8,4,64,1024]{3,2,1,0:T(8,128)(2,1)} async-done(((bf16[8,4,64,1024]{3,2,1,0:T(8,128)(2,1)}), bf16[8,4,64,1024]{3,2,1,0:T(8,128)(2,1)}, u32[]{:S(2)}, u32[]{:S(2)}) %all-to-all-start.2) | async-done | bytes 4194336 | tf_op jit(solution)/shard_map/all_to_all | solution.py:93
  193.5 4.5 copy.41
  198.0 4.6 fusion.4
  202.5 7.5 reshape.206
  210.0 6.8 add_convert_fusion
  217.1 3.1 fusion.12
  223.6 8.1 fusion.15
  231.7 60.6 %reduce-scatter.5.cloned.1.call-done = bf16[128,1024]{1,0:T(8,128)(2,1)} async-done(((bf16[2048,1024]{1,0:T(8,128)(2,1)}), bf16[128,1024]{1,0:T(8,128)(2,1)}) %reduce-scatter.5.cloned.1.call-update) | async-done | bytes 262160 | tf_op jit(solution)/shard_map/reduce_scatter | solution.py:119
  294.6 13.9 %add_bitcast_fusion = f32[4096,1024]{0,1:T(8,128)} fusion(f32[1024,4096]{1,0:T(8,128)} %fusion.15, bf16[128,1024]{1,0:T(8,128)(2,1)S(1)} %fusion.3, bf16[128,4096]{1,0:T(8,128)(2,1)S(1)} %copy-done.7), kind=kOutput, calls=%fused_computation.1 | convolution fusion | flops 1077936128 | bytes 34865152 | tf_op jit(solution)/shard_map/qd,qe->de/dot_general | solution.py:132
  308.4 17.5 %copy.39 = f32[4096,1024]{1,0:T(8,128)} copy(f32[4096,1024]{0,1:T(8,128)} %add_bitcast_fusion) | data formatting | bytes 33554432
  325.9 7.3 convolution_convert_fusion.1
  333.2 7.3 convolution_convert_fusion
  340.6 660.7 %reduce-scatter.7.cloned.1.call-done = f32[32,1024]{1,0:T(8,128)} async-done(((f32[4096,1024]{1,0:T(8,128)}), f32[32,1024]{1,0:T(8,128)}) %reduce-scatter.7.cloned.1.call-update) | async-done | bytes 131088
  (61 shorter events, 13.0 us)
Async XLA Ops:
  7.2 75.1 %copy-start = (bf16[128,4096]{1,0:T(8,128)(2,1)S(1)}, bf16[128,4096]{1,0:T(8,128)(2,1)}, u32[]{:S(2)}) copy-start(bf16[128,4096]{1,0:T(8,128)(2,1)} %param.5) | copy-start | bytes 3145732
  7.2 6.8 copy-start.9
  7.2 60.8 %all-gather.2.cloned.1.call-start = ((), (), s32[]{:S(2)}) async-start(), calls=%async_computation.5 | async-start | bytes 4456448 | tf_op jit(solution)/shard_map/all_gather | solution.py:35
  12.4 0.8 copy-start.3
  77.4 54.2 %all-to-all-start.1 = ((bf16[8,4,64,1024]{3,2,1,0:T(8,128)(2,1)}), bf16[8,4,64,1024]{3,2,1,0:T(8,128)(2,1)}, u32[]{:S(2)}, u32[]{:S(2)}) async-start(bf16[8,4,64,1024]{3,2,1,0:T(8,128)(2,1)} %broadcast_multiply_fusion), calls=%async_computation.1 | async-start | bytes 8388608 | tf_op jit(solution)/shard_map/all_to_all | solution.py:72
  82.3 4.9 copy-start.8
  82.3 5.8 copy-start.2
  87.1 0.8 copy-start.5
  139.2 54.2 %all-to-all-start.2 = ((bf16[8,4,64,1024]{3,2,1,0:T(8,128)(2,1)}), bf16[8,4,64,1024]{3,2,1,0:T(8,128)(2,1)}, u32[]{:S(2)}, u32[]{:S(2)}) async-start(bf16[8,4,64,1024]{3,2,1,0:T(8,128)(2,1)} %bitcast.58), calls=%async_computation.2 | async-start | bytes 8388608 | tf_op jit(solution)/shard_map/all_to_all | solution.py:93
  143.8 148.5 %reduce-scatter.5.cloned.1.call-start = ((), (), s32[]{:S(2)}) async-start(), calls=%async_computation.6 | async-start | bytes 4456448 | tf_op jit(solution)/shard_map/reduce_scatter | solution.py:119
  216.9 784.4 %reduce-scatter.7.cloned.1.call-start = ((), (), s32[]{:S(2)}) async-start(), calls=%async_computation.7 | async-start | bytes 16908288
  217.1 3.1 copy-start.6
  223.5 68.7 %copy-start.4 = (f32[128,1024]{1,0:T(8,128)S(1)}, f32[128,1024]{1,0:T(8,128)}, u32[]{:S(2)}) copy-start(f32[128,1024]{1,0:T(8,128)} %copy-done.3) | copy-start | bytes 1572868
  223.6 71.0 %copy-start.7 = (bf16[128,4096]{1,0:T(8,128)(2,1)S(1)}, bf16[128,4096]{1,0:T(8,128)(2,1)}, u32[]{:S(2)}) copy-start(bf16[128,4096]{1,0:T(8,128)(2,1)} %param.6) | copy-start | bytes 3145732
  325.9 675.4 %copy-start.1 = (bf16[128,4096]{1,0:T(8,128)(2,1)S(1)}, bf16[128,4096]{1,0:T(8,128)(2,1)}, u32[]{:S(2)}) copy-start(bf16[128,4096]{1,0:T(8,128)(2,1)} %param.5) | copy-start | bytes 3145732
Sparse Core Ops, SparseCore 0:
  14.1 53.8 all-gather.1
  217.0 75.2 reduce-scatter.4
  326.0 675.1 reduce-scatter.6
where the time goes:
time: 1010 us
  waiting for transfers between devices  854 us (85%)
  matrix products  72.9 us (7%)
  local copies, waits for them, and re-layouts  37.3 us (4%)
  between operations  14 us (1%)
  blocking collectives  10.5 us (1%)
    unnamed x4, waiting for transfers between devices  661 us
    reduce_scatter x1, waiting for transfers between devices, body(): lax.psum_scatter(code_terms.astype(jnp.bfloat16), 'member', scatter_dimen...  60.6 us
    all_to_all x1, waiting for transfers between devices, body(): lax.all_to_all(outgoing.reshape(groups, capacity, CB, emb_width), 'group'...  48.2 us
    all_gather x1, waiting for transfers between devices, body(): group_codes = lax.all_gather(c_emb, 'member', axis=0, tiled=True)  42.7 us
    all_to_all x1, waiting for transfers between devices, body(): lax.all_to_all(picked, 'group', split_axis=0, concat_axis=0, tiled=True)  42 us
    unnamed x22, local copies, waits for them, and re-layouts  23.6 us
  transfers between devices with their start and end apart: 5, of which 5 were waited for; matrix products, arithmetic and copies ran while one was open for 4% of the time, Pallas kernels for 0%

commit v1 on v0

--- a/solution.py
+++ b/solution.py
@@ -21,6 +21,16 @@
 
 
 def body(query_feat, code_feat, projection, hard_ids, loss_weight):
+
+    def mix_flows(slab_in):
+        placed = lax.all_to_all(
+            jnp.stack([slab_in] * lax.axis_size("member")),
+            axis_name="member",
+            split_axis=0,
+            concat_axis=0,
+        )
+        return jnp.concatenate(placed, axis=0)
+
     groups = lax.axis_size("group")
     members = lax.axis_size("member")
     member_index = lax.axis_index("member")
@@ -32,7 +42,7 @@
     capacity = 2 * count_hard // groups
     q_unit, q_inv, q_emb = embed(query_feat, projection)
     c_unit, c_inv, c_emb = embed(code_feat, projection)
-    group_codes = lax.all_gather(c_emb, "member", axis=0, tiled=True)
+    group_codes = mix_flows(c_emb)
     code_blocks = group_codes.reshape(per_group, CB, emb_width)
     wanted = hard_ids[0]
     owner_group = wanted // per_group

time: 1010 us -> 1040 us (1.030)
  waiting for transfers between devices: 854 us -> 873 us
  starting transfers between devices: 9.62 us -> 27 us
  blocking collectives: 10.5 us -> 0 us
    all_to_all x0 -> x2, waiting for transfers between devices: none -> 55.4 us  [the longest x1 55.4 us: mix_flows(): lax.all_to_all(jnp.stack([slab_in] * lax.axis_size('member')), axis_name=...]
    all_gather x1 -> x0, waiting for transfers between devices: 42.7 us -> none  [body(): group_codes = lax.all_gather(c_emb, 'member', axis=0, tiled=True)]
    all_to_all x0 -> x2, starting transfers between devices: none -> 12.5 us  [the longest x1 7.09 us: mix_flows(): lax.all_to_all(jnp.stack([slab_in] * lax.axis_size('member')), axis_name=...]
    all_to_all x1 -> x0, blocking collectives: 10.5 us -> none  [body(): lax.all_to_all(request_table, 'group', split_axis=0, concat_axis=0, tiled...]
    unnamed x4 -> x3, waiting for transfers between devices: 661 us -> 661 us
    unnamed x22 -> x18, local copies, waits for them, and re-layouts: 23.6 us -> 23.5 us
  transfers between devices with their start and end apart: 5 -> 6, of which waited for: 5 -> 5; matrix products, arithmetic and copies ran while one was open for 4% -> 4% of each run, Pallas kernels for 0% -> 0%
where the time goes in v1:
time: 1040 us
  waiting for transfers between devices  873 us (84%)
  matrix products  74.9 us (7%)
  local copies, waits for them, and re-layouts  40.3 us (4%)
  starting transfers between devices  27 us (3%)
  between operations  14.3 us (1%)
    unnamed x3, waiting for transfers between devices  661 us
    reduce_scatter x1, waiting for transfers between devices, body(): lax.psum_scatter(code_terms.astype(jnp.bfloat16), 'member', scatter_dimen...  68 us
    all_to_all x1, waiting for transfers between devices, mix_flows(): lax.all_to_all(jnp.stack([slab_in] * lax.axis_size('member')), axis_name=...  55.4 us
    all_to_all x1, waiting for transfers between devices, body(): lax.all_to_all(outgoing.reshape(groups, capacity, CB, emb_width), 'group'...  48.2 us
    all_to_all x1, waiting for transfers between devices, body(): lax.all_to_all(picked, 'group', split_axis=0, concat_axis=0, tiled=True)  40.2 us
    unnamed x18, local copies, waits for them, and re-layouts  23.5 us
  transfers between devices with their start and end apart: 6, of which 5 were waited for; matrix products, arithmetic and copies ran while one was open for 4% of the time, Pallas kernels for 0%

profile of v1, /device:TPU:0, one launch (start us, length us, event | category | flops | bytes accessed | tf_op | source)
XLA Modules:
  0.0 1039.3 jit_solution(14120673385267480988)
XLA Ops:
  9.6 5.4 all-to-all-start.1
  15.0 5.0 multiply_reduce_fusion.1
  23.5 7.1 all-to-all-start
  30.9 55.4 %all-to-all-done = bf16[16,128,1024]{2,1,0:T(8,128)(2,1)} async-done(((bf16[16,128,1024]{2,1,0:T(8,128)(2,1)}), bf16[16,128,1024]{2,1,0:T(8,128)(2,1)}, u32[]{:S(2)}, u32[]{:S(2)}) %all-to-all-start) | async-done | bytes 4194336 | tf_op jit(solution)/shard_map/all_to_all | solution.py:26
  86.3 5.0 gather_fusion
  91.3 4.5 broadcast_multiply_fusion
  95.7 9.5 all-to-all-start.2
  105.5 4.7 multiply_reduce_fusion.2
  111.0 3.8 fusion.13
  114.8 40.2 %all-to-all-done.2 = bf16[8,4,64,1024]{3,2,1,0:T(8,128)(2,1)} async-done(((bf16[8,4,64,1024]{3,2,1,0:T(8,128)(2,1)}), bf16[8,4,64,1024]{3,2,1,0:T(8,128)(2,1)}, u32[]{:S(2)}, u32[]{:S(2)}) %all-to-all-start.2) | async-done | bytes 4194336 | tf_op jit(solution)/shard_map/all_to_all | solution.py:82
  155.0 3.8 fusion.14
  162.6 4.5 all-to-all-start.3
  168.7 48.2 %all-to-all-done.3 = bf16[8,4,64,1024]{3,2,1,0:T(8,128)(2,1)} async-done(((bf16[8,4,64,1024]{3,2,1,0:T(8,128)(2,1)}), bf16[8,4,64,1024]{3,2,1,0:T(8,128)(2,1)}, u32[]{:S(2)}, u32[]{:S(2)}) %all-to-all-start.3) | async-done | bytes 4194336 | tf_op jit(solution)/shard_map/all_to_all | solution.py:103
  216.8 4.5 copy.41
  221.3 4.6 fusion.4
  225.9 7.5 reshape.208
  233.4 6.8 add_convert_fusion
  246.9 8.1 fusion.15
  255.1 68.0 %reduce-scatter.5.cloned.1.call-done = bf16[128,1024]{1,0:T(8,128)(2,1)} async-done(((bf16[2048,1024]{1,0:T(8,128)(2,1)}), bf16[128,1024]{1,0:T(8,128)(2,1)}) %reduce-scatter.5.cloned.1.call-update) | async-done | bytes 262160 | tf_op jit(solution)/shard_map/reduce_scatter | solution.py:129
  325.4 13.9 %add_bitcast_fusion = f32[4096,1024]{0,1:T(8,128)} fusion(f32[1024,4096]{1,0:T(8,128)} %fusion.15, bf16[128,1024]{1,0:T(8,128)(2,1)S(1)} %fusion.3, bf16[128,4096]{1,0:T(8,128)(2,1)S(1)} %copy-done.6), kind=kOutput, calls=%fused_computation.1 | convolution fusion | flops 1077936128 | bytes 34865152 | tf_op jit(solution)/shard_map/qd,qe->de/dot_general | solution.py:142
  339.2 17.5 %copy.39 = f32[4096,1024]{1,0:T(8,128)} copy(f32[4096,1024]{0,1:T(8,128)} %add_bitcast_fusion) | data formatting | bytes 33554432
  356.7 7.3 convolution_convert_fusion.1
  364.0 7.3 convolution_convert_fusion
  371.4 661.1 %reduce-scatter.7.cloned.1.call-done = f32[32,1024]{1,0:T(8,128)} async-done(((f32[4096,1024]{1,0:T(8,128)}), f32[32,1024]{1,0:T(8,128)}) %reduce-scatter.7.cloned.1.call-update) | async-done | bytes 131088
  (58 shorter events, 21.5 us)
Async XLA Ops:
  7.2 98.3 %copy-start = (bf16[128,4096]{1,0:T(8,128)(2,1)S(1)}, bf16[128,4096]{1,0:T(8,128)(2,1)}, u32[]{:S(2)}) copy-start(bf16[128,4096]{1,0:T(8,128)(2,1)} %param.5) | copy-start | bytes 3145732
  9.6 11.4 %all-to-all-start.1 = ((s32[8,1,4]{2,1,0:T(1,128)}), s32[8,1,4]{2,1,0:T(1,128)S(1)}, u32[]{:S(2)}, u32[]{:S(2)}) async-start(s32[8,1,4]{2,1,0:T(1,128)} %copy.33), calls=%async_computation.1 | async-start | bytes 8192 | tf_op jit(solution)/shard_map/all_to_all | solution.py:67
  20.1 0.8 copy-start.2
  23.5 62.9 %all-to-all-start = ((bf16[16,128,1024]{2,1,0:T(8,128)(2,1)}), bf16[16,128,1024]{2,1,0:T(8,128)(2,1)}, u32[]{:S(2)}, u32[]{:S(2)}) async-start(bf16[16,128,1024]{2,1,0:T(8,128)(2,1)} %stack.2), calls=%async_computation | async-start | bytes 8388608 | tf_op jit(solution)/shard_map/all_to_all | solution.py:26
  95.7 59.3 %all-to-all-start.2 = ((bf16[8,4,64,1024]{3,2,1,0:T(8,128)(2,1)}), bf16[8,4,64,1024]{3,2,1,0:T(8,128)(2,1)}, u32[]{:S(2)}, u32[]{:S(2)}) async-start(bf16[8,4,64,1024]{3,2,1,0:T(8,128)(2,1)} %broadcast_multiply_fusion), calls=%async_computation.2 | async-start | bytes 8388608 | tf_op jit(solution)/shard_map/all_to_all | solution.py:82
  105.5 4.7 copy-start.7
  110.2 0.8 copy-start.4
  162.6 54.2 %all-to-all-start.3 = ((bf16[8,4,64,1024]{3,2,1,0:T(8,128)(2,1)}), bf16[8,4,64,1024]{3,2,1,0:T(8,128)(2,1)}, u32[]{:S(2)}, u32[]{:S(2)}) async-start(bf16[8,4,64,1024]{3,2,1,0:T(8,128)(2,1)} %bitcast.58), calls=%async_computation.3 | async-start | bytes 8388608 | tf_op jit(solution)/shard_map/all_to_all | solution.py:103
  167.2 155.9 %reduce-scatter.5.cloned.1.call-start = ((), (), s32[]{:S(2)}) async-start(), calls=%async_computation.6 | async-start | bytes 4456448 | tf_op jit(solution)/shard_map/reduce_scatter | solution.py:129
  240.2 792.3 %reduce-scatter.7.cloned.1.call-start = ((), (), s32[]{:S(2)}) async-start(), calls=%async_computation.7 | async-start | bytes 16908288
  240.5 3.1 copy-start.5
  246.9 76.1 %copy-start.3 = (f32[128,1024]{1,0:T(8,128)S(1)}, f32[128,1024]{1,0:T(8,128)}, u32[]{:S(2)}) copy-start(f32[128,1024]{1,0:T(8,128)} %copy-done.2) | copy-start | bytes 1572868
  246.9 78.4 %copy-start.6 = (bf16[128,4096]{1,0:T(8,128)(2,1)S(1)}, bf16[128,4096]{1,0:T(8,128)(2,1)}, u32[]{:S(2)}) copy-start(bf16[128,4096]{1,0:T(8,128)(2,1)} %param.6) | copy-start | bytes 3145732
  356.7 675.8 %copy-start.1 = (bf16[128,4096]{1,0:T(8,128)(2,1)S(1)}, bf16[128,4096]{1,0:T(8,128)(2,1)}, u32[]{:S(2)}) copy-start(bf16[128,4096]{1,0:T(8,128)(2,1)} %param.5) | copy-start | bytes 3145732
Sparse Core Ops, SparseCore 0:
  240.3 82.6 reduce-scatter.4
  356.8 675.6 reduce-scatter.6
